TPU v7x, 32 devices: a whole 2x2x4 slice. The times are simulated.
32 devices in a mesh: dp: 4 (over y, x), label: 8 (over z, core).
Axes of the slice: x: 2, y: 2, z: 4, core: 2. Of those that a mesh axis runs over, the one named last changes fastest.
Arguments:
- encoded: bfloat16 [8192, 768], P(('dp', 'label')), may hold values from -8 to 8
- coarse_weight: bfloat16 [512, 768], P(('dp', 'label')), may hold values from -1 to 1
- fine_weight: bfloat16 [512, 128, 768], P(('dp', 'label')), may hold values from -0.21875 to 0.21875
- cluster_group: int32 [8192, 8], P(('dp', 'label')), may hold values from 0 to 31, all different within a row; in each aligned block of 256 rows (0 to 255, 256 to 511, ...) at most 96 rows name the same one
- cluster_member: int32 [8192, 8], P(('dp', 'label')), may hold values from 0 to 15
- positive: int32 [8192], P(('dp', 'label')), may hold values from 0 to 127
Outputs:
- row_loss: float32 [8192], P(('dp', 'label'))
- d_encoded: bfloat16 [8192, 768], P(('dp', 'label'))
- d_fine: bfloat16 [512, 128, 768], P(('dp', 'label'))
- cluster_loss: float32 [512], P(('dp', 'label'))
Inputs may be any that keep to these rules, and one draw needn't show every extreme that they name: `cluster_group`: each row names 8 different groups. Among the rows of one device (aligned blocks of 256 rows) no group is named by more than 96 rows, a bound that some block reaches.
All inputs are finite; a program needn't handle non-finite values.
Results may differ from a plain program's by a relative error of at most 0.0051.
Values may be sent and summed in bfloat16 or wider, within the bound.
A program may use at most 128 MiB of HBM per device.

v0:
```python
import jax
import jax.numpy as jnp
from jax import lax
from jax.sharding import PartitionSpec as P


def per_device(encoded, coarse_weight, fine_weight, cluster_group, cluster_member, positive):
    row_dev, features = encoded.shape
    own_clusters = coarse_weight.shape[0]
    labels = fine_weight.shape[1]
    per_row = cluster_group.shape[1]
    dp_size = lax.axis_size("dp")
    label_size = lax.axis_size("label")
    device_total = dp_size * label_size
    cluster = cluster_group * own_clusters + cluster_member
    target = cluster[:, 0]
    full_weight = lax.all_gather(coarse_weight, ("dp", "label"), axis=0, tiled=True)
    scores = jnp.dot(encoded, full_weight.T, preferred_element_type=jnp.float32)
    column_ids = jnp.arange(scores.shape[1], dtype=jnp.int32)
    is_target = column_ids[None, :] == target[:, None]
    top_score = jnp.max(scores, axis=1, keepdims=True)
    logsum = top_score[:, 0] + jnp.log(jnp.sum(jnp.exp(scores - top_score), axis=1))
    target_score = jnp.sum(jnp.where(is_target, scores, 0.0), axis=1)
    coarse_grad = (jnp.exp(scores - logsum[:, None]) - is_target.astype(jnp.float32)).astype(
        jnp.bfloat16
    )
    coarse_back = jnp.dot(coarse_grad, full_weight, preferred_element_type=jnp.float32)
    row_loss = logsum - target_score
    capacity = max(2, 3 * row_dev * per_row // (2 * device_total))
    slot_count = row_dev * per_row
    group_ids = jnp.arange(device_total, dtype=jnp.int32)
    group_hit = (cluster_group[:, :, None] == group_ids[None, None, :]).astype(jnp.bfloat16)
    row_hit = jnp.sum(group_hit, axis=1)
    row_index = jnp.arange(row_dev, dtype=jnp.int32)
    strictly_lower = (row_index[:, None] > row_index[None, :]).astype(jnp.bfloat16)
    earlier_rows = jnp.dot(strictly_lower, row_hit, preferred_element_type=jnp.float32).astype(
        jnp.int32
    )
    ranking = jnp.take_along_axis(earlier_rows, cluster_group, axis=1)
    slot_place = (cluster_group * capacity + ranking).reshape(slot_count)
    slot_total = device_total * capacity
    in_row = jnp.arange(slot_count, dtype=jnp.int32) % per_row
    row_of = jnp.arange(slot_count, dtype=jnp.int32) // per_row
    slot_truth = jnp.where(in_row == 0, positive[row_of], -1)
    send_rows = (
        jnp.zeros((slot_total, features), jnp.bfloat16)
        .at[slot_place]
        .set(jnp.repeat(encoded, per_row, axis=0))
    )
    send_member = (
        jnp.full((slot_total,), float(own_clusters), jnp.float32)
        .at[slot_place]
        .set(cluster_member.reshape(slot_count).astype(jnp.float32))
    )
    send_truth = (
        jnp.full((slot_total,), -1.0, jnp.float32)
        .at[slot_place]
        .set(slot_truth.astype(jnp.float32))
    )
    recv_rows, recv_member, recv_truth = (
        lax.all_to_all(
            lax.all_to_all(
                send_rows.reshape(dp_size, label_size, capacity, features),
                "dp",
                split_axis=0,
                concat_axis=0,
                tiled=True,
            ),
            "label",
            split_axis=1,
            concat_axis=1,
            tiled=True,
        ),
        lax.all_to_all(
            lax.all_to_all(
                send_member.astype(jnp.bfloat16).reshape(dp_size, label_size, capacity),
                "dp",
                split_axis=0,
                concat_axis=0,
                tiled=True,
            ),
            "label",
            split_axis=1,
            concat_axis=1,
            tiled=True,
        ),
        lax.all_to_all(
            lax.all_to_all(
                send_truth.astype(jnp.bfloat16).reshape(dp_size, label_size, capacity),
                "dp",
                split_axis=0,
                concat_axis=0,
                tiled=True,
            ),
            "label",
            split_axis=1,
            concat_axis=1,
            tiled=True,
        ),
    )
    in_rows = recv_rows.reshape(slot_total, features)
    in_member = recv_member.reshape(slot_total).astype(jnp.int32)
    in_truth = recv_truth.reshape(slot_total).astype(jnp.int32)
    window = min(128, slot_total)
    turns = own_clusters + (slot_total + window - 1) // window
    sorted_index = jnp.argsort(in_member, stable=True)
    member_ids = jnp.arange(own_clusters, dtype=jnp.int32)
    counts = jnp.sum((in_member[:, None] == member_ids[None, :]).astype(jnp.int32), axis=0)
    starts = jnp.cumsum(counts) - counts
    blocks_each = (counts + window - 1) // window
    block_end = jnp.cumsum(blocks_each)
    block_start = block_end - blocks_each
    sorted_rows = jnp.concatenate(
        [in_rows[sorted_index], jnp.zeros((window, features), jnp.bfloat16)], axis=0
    )
    sorted_truth = jnp.concatenate([in_truth[sorted_index], jnp.full((window,), -1, jnp.int32)])
    label_ids = jnp.arange(labels, dtype=jnp.int32)
    window_ids = jnp.arange(window, dtype=jnp.int32)

    def visit(visit_index, carry):
        back_rows, weight_grads, losses = carry
        cluster_now = jnp.sum((block_end <= visit_index).astype(jnp.int32))
        active = cluster_now < own_clusters
        clamped = jnp.minimum(cluster_now, own_clusters - 1)
        offset = (visit_index - block_start[clamped]) * window
        base_row = starts[clamped] + offset
        usable = active & (offset + window_ids < counts[clamped])
        rows_now = lax.dynamic_slice_in_dim(sorted_rows, base_row, window, 0)
        truth_ids = lax.dynamic_slice_in_dim(sorted_truth, base_row, window, 0)
        weight_now = lax.dynamic_index_in_dim(fine_weight, clamped, 0, keepdims=False)
        logits = jnp.dot(rows_now, weight_now.T, preferred_element_type=jnp.float32)
        truth = (truth_ids[:, None] == label_ids[None, :]).astype(jnp.float32)
        mask = usable[:, None].astype(jnp.float32)
        bce = jnp.maximum(logits, 0.0) + jnp.log1p(jnp.exp(-jnp.abs(logits))) - truth * logits
        loss_now = jnp.sum(bce * mask) / (per_row * labels)
        grad_now = ((jax.nn.sigmoid(logits) - truth) / per_row * mask).astype(jnp.bfloat16)
        back_now = jnp.dot(grad_now, weight_now, preferred_element_type=jnp.float32).astype(
            jnp.bfloat16
        )
        current = lax.dynamic_slice_in_dim(back_rows, base_row, window, 0)
        back_rows = lax.dynamic_update_slice_in_dim(back_rows, current + back_now, base_row, 0)
        weight_step = lax.dot_general(
            grad_now, rows_now, (((0,), (0,)), ((), ())), preferred_element_type=jnp.float32
        )
        weight_grads = weight_grads.at[clamped].add(weight_step)
        losses = losses.at[clamped].add(loss_now)
        return (back_rows, weight_grads, losses)

    start_carry = (
        jnp.zeros((slot_total + window, features), jnp.bfloat16),
        jnp.zeros((own_clusters, labels, features), jnp.float32),
        jnp.zeros((own_clusters,), jnp.float32),
    )
    back_rows, weight_grads, cluster_loss = lax.fori_loop(0, turns, visit, start_carry)
    d_fine = weight_grads.astype(jnp.bfloat16)
    back_slots = (
        jnp.zeros((slot_total, features), jnp.bfloat16).at[sorted_index].set(back_rows[:slot_total])
    )
    returned = lax.all_to_all(
        lax.all_to_all(
            back_slots.reshape(dp_size, label_size, capacity, features),
            "dp",
            split_axis=0,
            concat_axis=0,
            tiled=True,
        ),
        "label",
        split_axis=1,
        concat_axis=1,
        tiled=True,
    )
    slot_back = returned.reshape(slot_total, features)[slot_place]
    fine_sum = jnp.sum(slot_back.reshape(row_dev, per_row, features).astype(jnp.float32), axis=1)
    d_encoded = (coarse_back + fine_sum).astype(jnp.bfloat16)
    return (row_loss, d_encoded, d_fine, cluster_loss)


def solution(mesh):
    placed = (
        P(("dp", "label"), None),
        P(("dp", "label"), None),
        P(("dp", "label"), None, None),
        P(("dp", "label"), None),
        P(("dp", "label"), None),
        P(("dp", "label")),
    )
    return jax.shard_map(
        per_device,
        mesh=mesh,
        in_specs=placed,
        out_specs=(
            P(("dp", "label")),
            P(("dp", "label"), None),
            P(("dp", "label"), None, None),
            P(("dp", "label")),
        ),
        check_vma=False,
    )
```

profile of v0, /device:TPU:0, one launch (start us, length us, event | category | flops | bytes accessed | tf_op | source)
XLA Modules:
  0.0 1177.1 jit_solution(12285084408082046245)
XLA Ops:
  2.5 16.8 %gather_fusion.4 = s32[2048]{0:T(1024)S(1)} fusion(s32[256,32]{0,1:T(8,128)S(1)} %convolution_convert_fusion.1, s32[2048]{0:T(1024)S(1)} %reshape.380), kind=kCustom, calls=%fused_computation.4 | custom fusion | bytes 32768 | tf_op jit(solution)/shard_map/jit(take_along_axis)/gather | solution.py:39
  20.1 8.1 scatter_custom_fusion
  28.9 5.2 all-to-all-start
  34.1 13.1 %gather_fusion.1 = s32[2048]{0:T(1024)S(1)} fusion(s32[256]{0:T(256)S(1)} %copy-done.1, s32[2048]{0:T(1024)S(1)} %broadcast_clamp_fusion.2), kind=kCustom, calls=%fused_computation.1 | custom fusion | bytes 24576 | tf_op jit(solution)/shard_map/gather | solution.py:44
  47.2 8.1 scatter_custom_fusion.2
  64.9 4.9 all-to-all-start.1
  69.8 12.6 %scatter_custom_fusion.1 = bf16[3072,768]{1,0:T(8,128)(2,1)} fusion(s32[2048]{0:T(1024)S(1)} %bitcast.65, bf16[]{:T(256)} %constant.239.clone.1, bf16[256,768]{1,0:T(8,128)(2,1)S(1)} %copy-done), kind=kCustom, calls=%fused_computation.47 | custom fusion | bytes 5111810 | tf_op jit(solution)/shard_map/scatter | solution.py:48
  82.3 4.9 all-to-all-start.2
  87.9 53.4 %all-to-all-done.2 = bf16[4,8,96,768]{3,2,1,0:T(8,128)(2,1)} async-done(((bf16[4,8,96,768]{3,2,1,0:T(8,128)(2,1)}), bf16[4,8,96,768]{3,2,1,0:T(8,128)(2,1)}, u32[]{:S(2)}, u32[]{:S(2)}) %all-to-all-start.2) | async-done | bytes 4718624 | tf_op jit(solution)/shard_map/all_to_all | solution.py:62
  146.0 4.9 copy.82
  151.6 4.8 all-to-all-start.3
  157.1 5.8 sort.17
  162.9 17.4 %gather_fusion.2 = s32[3072]{0:T(1024)S(1)} fusion(s32[3072]{0:T(1024)S(1)} %reshape.346, s32[3072]{0:T(1024)S(1)} %get-tuple-element.359), kind=kCustom, calls=%fused_computation.2 | custom fusion | bytes 36864 | tf_op jit(solution)/shard_map/gather | solution.py:116
  180.4 81.0 %all-to-all-done.3 = bf16[4,8,96,768]{3,2,0,1:T(8,128)(2,1)} async-done(((bf16[4,8,96,768]{3,2,0,1:T(8,128)(2,1)}), bf16[4,8,96,768]{3,2,0,1:T(8,128)(2,1)}, u32[]{:S(2)}, u32[]{:S(2)}) %all-to-all-start.3) | async-done | bytes 4718624 | tf_op jit(solution)/shard_map/all_to_all | solution.py:61
  261.4 4.9 copy.83
  266.3 17.5 %gather_fusion = bf16[3072,768]{1,0:T(8,128)(2,1)} fusion(bf16[3072,768]{1,0:T(8,128)(2,1)} %bitcast.59, s32[3072]{0:T(1024)S(1)} %get-tuple-element.359), kind=kCustom, calls=%fused_computation | custom fusion | bytes 9449472 | tf_op jit(solution)/shard_map/gather | solution.py:114
  283.8 4.9 concatenate.18
  294.6 633.4 %while.22 = (s32[]{:T(128)}, bf16[3200,768]{1,0:T(8,128)(2,1)}, f32[16,128,768]{2,1,0:T(8,128)}, f32[16]{0:T(128)S(1)}, s32[16]{0:T(128)S(1)}, /*index=5*/s32[16...) while((s32[]{:T(128)}, bf16[3200,768]{1,0:T(8,128)(2,1)}, ...), condition=%wide.region_15.16_spmd.clone.clone, body=%wide.region_11.15_spmd.clone.clone.sunk | while | flops 76596312 | bytes 2563701 | solution.py:154
  928.0 17.6 %scatter_custom_fusion.3 = bf16[3072,768]{1,0:T(8,128)(2,1)} fusion(s32[3072]{0:T(1024)S(1)} %get-tuple-element.360, bf16[3200,768]{1,0:T(8,128)(2,1)} %get-tuple-element.276, bf16[]{:T(256)} %constant.239.clone.1), kind=kCustom, calls=%fused_computation.45 | custom fusion | bytes 9437696 | tf_op jit(solution)/shard_map/scatter | solution.py:157
  945.6 57.1 %all_to_all.40 = bf16[4,8,96,768]{3,2,1,0:T(8,128)(2,1)S(1)} all-to-all(bf16[4,8,96,768]{3,2,1,0:T(8,128)(2,1)} %bitcast.62), channel_id=1, replica_groups=mesh['dp'=4,'label'=8] {'dp'}, dimensions={0} | all-to-all | bytes 9437184 | tf_op jit(solution)/shard_map/all_to_all | solution.py:160
  1010.0 138.4 %all_gather.3 = bf16[512,768]{1,0:T(8,128)(2,1)S(1)} all-gather(bf16[16,768]{1,0:T(8,128)(2,1)S(1)} %copy-done.5), channel_id=1, replica_groups=mesh['dp'=4,'label'=8] {'dp','label'}, dimensions={0}, use_global_device_ids=true | all-gather | bytes 811008 | tf_op jit(solution)/shard_map/all_gather | solution.py:17
  1151.5 4.8 convert_element_type.123
  1156.3 4.8 copy.87
  1161.1 11.4 gather_fusion.3
  (596 shorter events, 542.1 us)
Async XLA Ops:
  0.6 69.1 %copy-start = (bf16[256,768]{1,0:T(8,128)(2,1)S(1)}, bf16[256,768]{1,0:T(8,128)(2,1)}, u32[]{:S(2)}) copy-start(bf16[256,768]{1,0:T(8,128)(2,1)} %param.12) | copy-start | bytes 1179652
  2.5 17.0 %copy-start.4 = (s32[256,8]{0,1:T(8,128)S(1)}, s32[256,8]{0,1:T(8,128)}, u32[]{:S(2)}) copy-start(s32[256,8]{0,1:T(8,128)} %param.15) | copy-start | bytes 24580
  2.5 17.3 %copy-start.8 = (s32[256,8]{0,1:T(8,128)S(1)}, s32[256,8]{0,1:T(8,128)}, u32[]{:S(2)}) copy-start(s32[256,8]{0,1:T(8,128)} %param.16) | copy-start | bytes 24580
  19.4 14.7 %copy-start.1 = (s32[256]{0:T(256)S(1)}, s32[256]{0:T(256)}, u32[]{:S(2)}) copy-start(s32[256]{0:T(256)} %param.17) | copy-start | bytes 3076
  28.9 27.1 %all-to-all-start = ((bf16[4,8,96]{2,1,0:T(8,128)(2,1)}), bf16[4,8,96]{2,1,0:T(8,128)(2,1)S(1)}, u32[]{:S(2)}, u32[]{:S(2)}) async-start(bf16[4,8,96]{2,1,0:T(8,128)(2,1)} %reshape.334), calls=%async_computation | async-start | bytes 16384 | tf_op jit(solution)/shard_map/all_to_all | solution.py:75
  56.0 8.9 all-to-all-start.4
  64.9 17.5 %all-to-all-start.1 = ((bf16[4,8,96]{2,0,1:T(4,128)(2,1)}), bf16[4,8,96]{2,0,1:T(4,128)(2,1)S(1)}, u32[]{:S(2)}, u32[]{:S(2)}) async-start(bf16[4,8,96]{2,0,1:T(4,128)(2,1)} %copy.78), calls=%async_computation.1 | async-start | bytes 16384 | tf_op jit(solution)/shard_map/all_to_all | solution.py:74
  82.3 58.9 %all-to-all-start.2 = ((bf16[4,8,96,768]{3,2,1,0:T(8,128)(2,1)}), bf16[4,8,96,768]{3,2,1,0:T(8,128)(2,1)}, u32[]{:S(2)}, u32[]{:S(2)}) async-start(bf16[4,8,96,768]{3,2,1,0:T(8,128)(2,1)} %bitcast.61), calls=%async_computation.2 | async-start | bytes 9437184 | tf_op jit(solution)/shard_map/all_to_all | solution.py:62
  141.2 10.3 all-to-all-start.5
  151.6 109.8 %all-to-all-start.3 = ((bf16[4,8,96,768]{3,2,0,1:T(8,128)(2,1)}), bf16[4,8,96,768]{3,2,0,1:T(8,128)(2,1)}, u32[]{:S(2)}, u32[]{:S(2)}) async-start(bf16[4,8,96,768]{3,2,0,1:T(8,128)(2,1)} %copy.82), calls=%async_computation.3 | async-start | bytes 9437184 | tf_op jit(solution)/shard_map/all_to_all | solution.py:61
  288.7 5.9 copy-start.7
  928.0 17.6 %copy-start.6 = (f32[16]{0:T(128)}, f32[16]{0:T(128)S(1)}, u32[]{:S(2)}) copy-start(f32[16]{0:T(128)S(1)} %get-tuple-element.274) | copy-start | bytes 196
  1005.2 4.8 copy-start.5
  1005.2 151.1 %all-to-all-start.7 = ((bf16[4,8,96,768]{3,2,0,1:T(8,128)(2,1)}), bf16[4,8,96,768]{3,2,0,1:T(8,128)(2,1)}, u32[]{:S(2)}, u32[]{:S(2)}) async-start(bf16[4,8,96,768]{3,2,0,1:T(8,128)(2,1)} %copy.86), calls=%async_computation.7 | async-start | bytes 9437184 | tf_op jit(solution)/shard_map/all_to_all | solution.py:159
  1148.4 0.9 copy-start.2
  1149.8 0.8 copy-start.3
where the time goes:
time: 1180 us
  local copies, waits for them, and re-layouts  304 us (26%)
  matrix products  244 us (21%)
  blocking collectives  195 us (17%)
  waiting for transfers between devices  139 us (12%)
  loops' own time  132 us (11%)
  other arithmetic  128 us (11%)
  starting transfers between devices  33.4 us (3%)
    all_gather x1, blocking collectives, per_device(): lax.all_gather(coarse_weight, ('dp', 'label'), axis=0, tiled=True)  138 us
    another operation x1, loops' own time, per_device(): lax.fori_loop(0, turns, visit, start_carry)  132 us
    dot_general x40, matrix products, visit(): lax.dot_general(grad_now, rows_now, (((0,), (0,)), ((), ())), preferred_e...  114 us
    all_to_all x1, waiting for transfers between devices, per_device(): lax.all_to_all(lax.all_to_all(send_rows.reshape(dp_size, label_size, capa...  81 us
    dot_general x40, matrix products, visit(): logits = jnp.dot(rows_now, weight_now.T, preferred_element_type=jnp.float32)  75.7 us
    dynamic_update_slice x40, local copies, waits for them, and re-layouts, visit(): lax.dynamic_update_slice_in_dim(back_rows, current + back_now, base_row, 0)  74.4 us
    all_to_all x1, blocking collectives, per_device(): lax.all_to_all(back_slots.reshape(dp_size, label_size, capacity, features...  57.1 us
    all_to_all x1, waiting for transfers between devices, per_device(): lax.all_to_all(send_rows.reshape(dp_size, label_size, capacity, features)...  53.4 us
  transfers between devices with their start and end apart: 7, of which 4 were waited for; matrix products, arithmetic and copies ran while one was open for 6% of the time, Pallas kernels for 0%

commit v1 on v0

--- a/solution.py
+++ b/solution.py
@@ -1,10 +1,14 @@
+import functools
+
 import jax
 import jax.numpy as jnp
 from jax import lax
+from jax.experimental import pallas as pl
+from jax.experimental.pallas import tpu as pltpu
 from jax.sharding import PartitionSpec as P
 
 
-def per_device(encoded, coarse_weight, fine_weight, cluster_group, cluster_member, positive):
+def per_device_exchange(encoded, coarse_weight, fine_weight, cluster_group, cluster_member, positive):
     row_dev, features = encoded.shape
     own_clusters = coarse_weight.shape[0]
     labels = fine_weight.shape[1]
@@ -175,6 +179,203 @@
     return (row_loss, d_encoded, d_fine, cluster_loss)
 
 
+SOURCES = 8
+
+
+def fine_kernel(capacity, labels, me_ref, upper_ref, gathered_ref, weight_ref, part_ref, dfine_ref,
+                loss_ref, sel, pick, member, truth, grad, back, total):
+    step = pl.program_id(0)
+    rows = part_ref.shape[1]
+    features = part_ref.shape[2]
+    slots = sel.shape[0]
+    meta_at = gathered_ref.shape[1] - 16
+    clusters = weight_ref.shape[0] // labels
+    per_row = 8
+
+    @pl.when(step == 0)
+    def _():
+        total[...] = jnp.zeros_like(total)
+        loss_ref[...] = jnp.zeros_like(loss_ref)
+
+    me = me_ref[0].astype(jnp.float32)
+    hits, members, truths = [], [], []
+    for i in range(SOURCES):
+        meta = gathered_ref[i, meta_at:, :].astype(jnp.float32)
+        hit = (meta[0:per_row, 0:rows] == me).astype(jnp.float32)
+        hits.append(jnp.sum(hit, axis=0, keepdims=True))
+        members.append(
+            jnp.sum(hit * (meta[0:per_row, rows : 2 * rows] + 1.0), axis=0, keepdims=True)
+        )
+        truths.append(hit[0:1] * (meta[0:1, 2 * rows : 3 * rows] + 1.0))
+    named = jnp.concatenate(hits, axis=0)
+    rank = jnp.dot(named.astype(jnp.bfloat16), upper_ref[...], preferred_element_type=jnp.float32)
+    rank = jnp.where(named > 0.0, rank, -1.0)
+    place = lax.broadcasted_iota(jnp.int32, (capacity, rows), 0).astype(jnp.float32)
+    for i in range(SOURCES):
+        at = pl.ds(i * capacity, capacity)
+        hot = (place == rank[i : i + 1, :]).astype(jnp.float32)
+        pick[at, :] = hot.astype(jnp.bfloat16)
+        sel[at, :] = jnp.dot(
+            hot.astype(jnp.bfloat16), gathered_ref[i, 0:rows, :], preferred_element_type=jnp.float32
+        ).astype(jnp.bfloat16)
+        member[at, :] = jnp.broadcast_to(
+            jnp.sum(hot * members[i], axis=1, keepdims=True) - 1.0, (capacity, labels)
+        )
+        truth[at, :] = jnp.broadcast_to(
+            jnp.sum(hot * truths[i], axis=1, keepdims=True) - 1.0, (capacity, labels)
+        )
+
+    grad[...] = jnp.zeros_like(grad)
+
+    @pl.loop(0, clusters // 2)
+    def _(pair):
+        first = (2 * pair).astype(jnp.float32)
+        w = weight_ref[pl.ds(pl.multiple_of(pair * 2 * labels, 2 * labels), 2 * labels), :]
+        both = lax.dot_general(
+            sel[...], w, (((1,), (1,)), ((), ())), preferred_element_type=jnp.float32
+        )
+        mine = member[...]
+        grad[...] = jnp.where(
+            mine == first,
+            both[:, :labels],
+            jnp.where(mine == first + 1.0, both[:, labels:], grad[...]),
+        )
+
+    logits = grad[...]
+    lane = lax.broadcasted_iota(jnp.int32, (slots, labels), 1).astype(jnp.float32)
+    is_true = (lane == truth[...]).astype(jnp.float32)
+    small = jnp.exp(-jnp.abs(logits))
+    inverse = 1.0 / (1.0 + small)
+    bce = jnp.maximum(logits, 0.0) + jnp.log1p(small) - is_true * logits
+    row_bce = jnp.sum(bce, axis=1, keepdims=True)
+    loss_ref[...] += jnp.sum(
+        jnp.where(lane == member[...], row_bce, 0.0), axis=0, keepdims=True
+    ) / (per_row * labels)
+    grad[...] = (jnp.where(logits >= 0.0, inverse, small * inverse) - is_true) / per_row
+    back[...] = jnp.zeros_like(back)
+
+    @pl.loop(0, clusters // 2)
+    def _(pair):
+        first = (2 * pair).astype(jnp.float32)
+        at = pl.ds(pl.multiple_of(pair * 2 * labels, 2 * labels), 2 * labels)
+        mine = member[...]
+        both = jnp.concatenate(
+            [
+                jnp.where(mine == first, grad[...], 0.0),
+                jnp.where(mine == first + 1.0, grad[...], 0.0),
+            ],
+            axis=1,
+        ).astype(jnp.bfloat16)
+        back[...] += jnp.dot(both, weight_ref[at, :], preferred_element_type=jnp.float32)
+        total[at, :] += lax.dot_general(
+            both, sel[...], (((0,), (0,)), ((), ())), preferred_element_type=jnp.float32
+        )
+
+    for i in range(SOURCES):
+        at = pl.ds(i * capacity, capacity)
+        part_ref[i] = lax.dot_general(
+            pick[at, :],
+            back[at, :].astype(jnp.bfloat16),
+            (((0,), (0,)), ((), ())),
+            preferred_element_type=jnp.float32,
+        ).astype(jnp.bfloat16)
+
+    @pl.when(step == pl.num_programs(0) - 1)
+    def _():
+        dfine_ref[...] = total[...].astype(jnp.bfloat16)
+
+
+def fine_part(gathered, fine_weight, me, rows, capacity):
+    device_total, height, features = gathered.shape
+    clusters, labels, _ = fine_weight.shape
+    slots = SOURCES * capacity
+    position = jnp.arange(rows, dtype=jnp.int32)
+    upper = (position[:, None] < position[None, :]).astype(jnp.bfloat16)
+    part, d_fine, loss = pl.pallas_call(
+        functools.partial(fine_kernel, capacity, labels),
+        grid=(device_total // SOURCES,),
+        in_specs=[
+            pl.BlockSpec(memory_space=pltpu.SMEM),
+            pl.BlockSpec((rows, rows), lambda s: (0, 0)),
+            pl.BlockSpec((SOURCES, height, features), lambda s: (s, 0, 0)),
+            pl.BlockSpec((clusters * labels, features), lambda s: (0, 0)),
+        ],
+        out_specs=[
+            pl.BlockSpec((SOURCES, rows, features), lambda s: (s, 0, 0)),
+            pl.BlockSpec((clusters * labels, features), lambda s: (0, 0)),
+            pl.BlockSpec((1, labels), lambda s: (0, 0)),
+        ],
+        out_shape=[
+            jax.ShapeDtypeStruct((device_total, rows, features), jnp.bfloat16),
+            jax.ShapeDtypeStruct((clusters * labels, features), jnp.bfloat16),
+            jax.ShapeDtypeStruct((1, labels), jnp.float32),
+        ],
+        scratch_shapes=[
+            pltpu.VMEM((slots, features), jnp.bfloat16),
+            pltpu.VMEM((slots, rows), jnp.bfloat16),
+            pltpu.VMEM((slots, labels), jnp.float32),
+            pltpu.VMEM((slots, labels), jnp.float32),
+            pltpu.VMEM((slots, labels), jnp.float32),
+            pltpu.VMEM((slots, features), jnp.float32),
+            pltpu.VMEM((clusters * labels, features), jnp.float32),
+        ],
+        compiler_params=pltpu.CompilerParams(vmem_limit_bytes=56 * 1024 * 1024),
+        name="fine_part",
+    )(me.reshape(1), upper, gathered, fine_weight.reshape(clusters * labels, features))
+    return part, d_fine.reshape(clusters, labels, features), loss[0, :clusters]
+
+
+def per_device_gather(encoded, coarse_weight, fine_weight, cluster_group, cluster_member, positive):
+    rows, features = encoded.shape
+    own_clusters = coarse_weight.shape[0]
+    per_row = cluster_group.shape[1]
+    device_total = lax.axis_size("dp") * lax.axis_size("label")
+    me = lax.axis_index("dp") * lax.axis_size("label") + lax.axis_index("label")
+    capacity = max(2, 3 * rows * per_row // (2 * device_total))
+    meta = jnp.concatenate(
+        [
+            cluster_group.T,
+            cluster_member.T,
+            jnp.broadcast_to(positive[None, :], (per_row, rows)),
+        ],
+        axis=1,
+    ).astype(jnp.bfloat16)
+    meta = jnp.pad(meta, ((0, 16 - per_row), (0, features - 3 * rows)))
+    block = jnp.concatenate([encoded, coarse_weight, meta], axis=0)
+    gathered = collect(block)
+    part, d_fine, cluster_loss = fine_part(gathered, fine_weight, me, rows, capacity)
+    fine_sum = send_back(part)
+    full_weight = gathered[:, rows : rows + own_clusters, :].reshape(-1, features)
+    target = cluster_group[:, 0] * own_clusters + cluster_member[:, 0]
+    scores = jnp.dot(encoded, full_weight.T, preferred_element_type=jnp.float32)
+    column_ids = jnp.arange(scores.shape[1], dtype=jnp.int32)
+    is_target = column_ids[None, :] == target[:, None]
+    top_score = jnp.max(scores, axis=1, keepdims=True)
+    logsum = top_score[:, 0] + jnp.log(jnp.sum(jnp.exp(scores - top_score), axis=1))
+    target_score = jnp.sum(jnp.where(is_target, scores, 0.0), axis=1)
+    coarse_grad = (jnp.exp(scores - logsum[:, None]) - is_target.astype(jnp.float32)).astype(
+        jnp.bfloat16
+    )
+    coarse_back = jnp.dot(coarse_grad, full_weight, preferred_element_type=jnp.float32)
+    d_encoded = (coarse_back + fine_sum.astype(jnp.float32)).astype(jnp.bfloat16)
+    return logsum - target_score, d_encoded, d_fine, cluster_loss
+
+
+def collect(block):
+    return lax.all_gather(block, ("dp", "label"), axis=0, tiled=False)
+
+
+def send_back(part):
+    return lax.psum_scatter(part, ("dp", "label"), scatter_dimension=0, tiled=False)
+
+
+def per_device(encoded, coarse_weight, fine_weight, cluster_group, cluster_member, positive):
+    device_total = lax.axis_size("dp") * lax.axis_size("label")
+    fits = device_total == 32 and encoded.shape[0] * 3 <= encoded.shape[1]
+    plan = per_device_gather if fits else per_device_exchange
+    return plan(encoded, coarse_weight, fine_weight, cluster_group, cluster_member, positive)
+
+
 def solution(mesh):
     placed = (
         P(("dp", "label"), None),

time: 1180 us -> 339 us (0.29)
  local copies, waits for them, and re-layouts: 304 us -> 1.72 us
  matrix products: 244 us -> 2.57 us
  blocking collectives: 195 us -> 0 us
  loops' own time: 132 us -> 0 us
  other arithmetic: 128 us -> 5.34 us
  waiting for transfers between devices: 139 us -> 257 us
  Pallas kernels: 0 us -> 58.2 us
  starting transfers between devices: 33.4 us -> 0.08 us
  between operations: 0.93 us -> 14.1 us
    dot_general x123 -> x2, matrix products: 244 us -> 2.57 us  [the longest x1 2.16 us: per_device_gather(): jnp.dot(coarse_grad, full_weight, preferred_element_type=jnp.float32)]
    reduce_scatter x0 -> x1, waiting for transfers between devices: none -> 150 us  [send_back(): lax.psum_scatter(part, ('dp', 'label'), scatter_dimension=0, tiled=False)]
    all_to_all x7 -> x0, waiting for transfers between devices: 139 us -> none  [the longest x1 81 us: per_device(): lax.all_to_all(lax.all_to_all(send_rows.reshape(dp_size, label_size, capa...]
    all_gather x1 -> x0, blocking collectives: 138 us -> none  [per_device(): lax.all_gather(coarse_weight, ('dp', 'label'), axis=0, tiled=True)]
    another operation x1 -> x0, loops' own time: 132 us -> none  [per_device(): lax.fori_loop(0, turns, visit, start_carry)]
    all_gather x0 -> x1, waiting for transfers between devices: none -> 106 us  [collect(): return lax.all_gather(block, ('dp', 'label'), axis=0, tiled=False)]
    gather x9 -> x0, local copies, waits for them, and re-layouts: 76.6 us -> none  [the longest x1 17.5 us: per_device(): in_rows[sorted_index]]
    dynamic_update_slice x40 -> x0, local copies, waits for them, and re-layouts: 74.4 us -> none  [visit(): lax.dynamic_update_slice_in_dim(back_rows, current + back_now, base_row, 0)]
  transfers between devices with their start and end apart: 7 -> 2, of which waited for: 4 -> 2; matrix products, arithmetic and copies ran while one was open for 6% -> 1% of each run, Pallas kernels for 0% -> 0%
where the time goes in v1:
time: 339 us; the launch traced here: 338 us
  waiting for transfers between devices  257 us (76%)
  Pallas kernels  58.2 us (17%)
  between operations  14.1 us (4%)
  other arithmetic  5.34 us (2%)
    reduce_scatter x1, waiting for transfers between devices, send_back(): lax.psum_scatter(part, ('dp', 'label'), scatter_dimension=0, tiled=False)  150 us
    all_gather x1, waiting for transfers between devices, collect(): return lax.all_gather(block, ('dp', 'label'), axis=0, tiled=False)  106 us
    pallas_call x1, Pallas kernels, fine_part(): pl.pallas_call(functools.partial(fine_kernel, capacity, labels), grid=(de...  58.2 us
  transfers between devices with their start and end apart: 2, of which 2 were waited for; matrix products, arithmetic and copies ran while one was open for 1% of the time, Pallas kernels for 0%

profile of v1, /device:TPU:0, one launch (start us, length us, event | category | flops | bytes accessed | tf_op | source)
XLA Modules:
  0.0 338.5 jit_solution(2373882279392139579)
XLA Ops:
  7.2 0.0 all-gather.3.cloned.1.call-start
  7.2 0.7 convert.15
  7.9 0.7 convert_bitcast_fusion
  8.6 1.8 fusion.8
  10.4 0.0 all-gather.3.cloned.1.call-update
  10.5 0.0 reduce-scatter.2.cloned.1.call-start
  10.5 0.7 fusion.12.upper_ref
  11.2 106.4 %all-gather.3.cloned.1.call-done = bf16[9216,768]{1,0:T(8,128)(2,1)} async-done(((bf16[288,768]{1,0:T(8,128)(2,1)}), bf16[9216,768]{1,0:T(8,128)(2,1)}) %all-gather.3.cloned.1.call-update) | async-done | bytes 14155792 | tf_op jit(solution)/shard_map/all_gather | solution.py:365
  117.6 0.0 copy-start
  117.6 58.2 %fine_part.1 = (bf16[32,256,768]{2,1,0:T(8,128)(2,1)}, bf16[2048,768]{1,0:T(8,128)(2,1)}, f32[1,128]{1,0:T(1,128)}) custom-call(s32[1]{0:T(128)} %bitcast.6.me_ref, bf16[256,256]{1,0:T(8,128)(2,1)} %fusion.12.upper_ref, bf16[32,288,768]{2,1,0:T(8,128)(2,1)} %bitcast.35, bf16[2048,768]{1,0:T(8,128)(2,1)} %bitcast.39), custom_call_target="tpu_custom_call" | custom-call | tf_op jit(solution)/shard_map/fine_part/pallas_call | solution.py:294
  175.8 0.0 copy-start.1
  175.8 0.0 reduce-scatter.2.cloned.1.call-update
  175.8 0.7 slice_add_fusion
  176.6 1.2 slice.16
  177.7 0.0 copy-done
  177.8 0.4 fusion.14
  178.2 0.2 fusion.4
  178.3 0.0 copy-done.1
  178.3 0.5 slice_bitcast_fusion
  178.9 0.6 fusion.13
  179.4 150.1 %reduce-scatter.2.cloned.1.call-done = bf16[1,256,768]{2,1,0:T(8,128)(2,1)} async-done(((bf16[32,256,768]{2,1,0:T(8,128)(2,1)}), bf16[1,256,768]{2,1,0:T(8,128)(2,1)}) %reduce-scatter.2.cloned.1.call-update) | async-done | bytes 393232 | tf_op jit(solution)/shard_map/reduce_scatter | solution.py:369
  329.5 2.2 fusion
  (2 shorter events, 0.0 us)
Async XLA Ops:
  7.2 110.4 %all-gather.3.cloned.1.call-start = ((), (), s32[]{:S(2)}) async-start(), calls=%async_computation.2 | async-start | bytes 14598144 | tf_op jit(solution)/shard_map/all_gather | solution.py:365
  10.5 319.0 %reduce-scatter.2.cloned.1.call-start = ((), (), s32[]{:S(2)}) async-start(), calls=%async_computation.1 | async-start | bytes 12976128 | tf_op jit(solution)/shard_map/reduce_scatter | solution.py:369
  117.6 60.1 %copy-start = (bf16[256,768]{1,0:T(8,128)(2,1)S(1)}, bf16[256,768]{1,0:T(8,128)(2,1)}, u32[]{:S(2)}) copy-start(bf16[256,768]{1,0:T(8,128)(2,1)} %param.6) | copy-start | bytes 1179652
  175.8 2.5 copy-start.1
Sparse Core Ops, SparseCore 0:
  11.6 105.9 all-gather.2
  176.0 153.4 reduce-scatter.1

commit v2 on v1

--- a/solution.py
+++ b/solution.py
@@ -180,6 +180,7 @@
 
 
 SOURCES = 8
+TOGETHER = 8
 
 
 def fine_kernel(capacity, labels, me_ref, upper_ref, gathered_ref, weight_ref, part_ref, dfine_ref,
@@ -227,19 +228,20 @@
 
     grad[...] = jnp.zeros_like(grad)
 
-    @pl.loop(0, clusters // 2)
-    def _(pair):
-        first = (2 * pair).astype(jnp.float32)
-        w = weight_ref[pl.ds(pl.multiple_of(pair * 2 * labels, 2 * labels), 2 * labels), :]
-        both = lax.dot_general(
+    span = TOGETHER * labels
+
+    @pl.loop(0, clusters // TOGETHER)
+    def _(group):
+        first = (TOGETHER * group).astype(jnp.float32)
+        w = weight_ref[pl.ds(pl.multiple_of(group * span, span), span), :]
+        every = lax.dot_general(
             sel[...], w, (((1,), (1,)), ((), ())), preferred_element_type=jnp.float32
         )
         mine = member[...]
-        grad[...] = jnp.where(
-            mine == first,
-            both[:, :labels],
-            jnp.where(mine == first + 1.0, both[:, labels:], grad[...]),
-        )
+        kept = grad[...]
+        for j in range(TOGETHER):
+            kept = jnp.where(mine == first + j, every[:, j * labels : (j + 1) * labels], kept)
+        grad[...] = kept
 
     logits = grad[...]
     lane = lax.broadcasted_iota(jnp.int32, (slots, labels), 1).astype(jnp.float32)
@@ -254,21 +256,18 @@
     grad[...] = (jnp.where(logits >= 0.0, inverse, small * inverse) - is_true) / per_row
     back[...] = jnp.zeros_like(back)
 
-    @pl.loop(0, clusters // 2)
-    def _(pair):
-        first = (2 * pair).astype(jnp.float32)
-        at = pl.ds(pl.multiple_of(pair * 2 * labels, 2 * labels), 2 * labels)
+    @pl.loop(0, clusters // TOGETHER)
+    def _(group):
+        first = (TOGETHER * group).astype(jnp.float32)
+        at = pl.ds(pl.multiple_of(group * span, span), span)
         mine = member[...]
-        both = jnp.concatenate(
-            [
-                jnp.where(mine == first, grad[...], 0.0),
-                jnp.where(mine == first + 1.0, grad[...], 0.0),
-            ],
-            axis=1,
+        own = grad[...]
+        every = jnp.concatenate(
+            [jnp.where(mine == first + j, own, 0.0) for j in range(TOGETHER)], axis=1
         ).astype(jnp.bfloat16)
-        back[...] += jnp.dot(both, weight_ref[at, :], preferred_element_type=jnp.float32)
+        back[...] += jnp.dot(every, weight_ref[at, :], preferred_element_type=jnp.float32)
         total[at, :] += lax.dot_general(
-            both, sel[...], (((0,), (0,)), ((), ())), preferred_element_type=jnp.float32
+            every, sel[...], (((0,), (0,)), ((), ())), preferred_element_type=jnp.float32
         )
 
     for i in range(SOURCES):
@@ -361,12 +360,332 @@
     return logsum - target_score, d_encoded, d_fine, cluster_loss
 
 
+MESH = pl.DeviceIdType.MESH
+
+
+class Around:
+    def __init__(self):
+        self.dp = lax.axis_index("dp")
+        self.label = lax.axis_index("label")
+        self.z = self.label // 2
+        self.core = self.label % 2
+        self.depth = lax.axis_size("label") // 2
+        self.line = (self.dp // 2) * 2 + 1 - self.dp % 2
+        self.column = (1 - self.dp // 2) * 2 + self.dp % 2
+        self.corner = 3 - self.dp
+        self.x = (self.line, self.label)
+        self.y = (self.column, self.label)
+        self.sibling = (self.dp, self.z * 2 + 1 - self.core)
+        self.left = (self.dp, self.label - 2)
+        self.right = (self.dp, self.label + 2)
+        self.has_left = self.z > 0
+        self.has_right = self.z < self.depth - 1
+        self.pending = []
+
+    def greet(self):
+        barrier = pltpu.get_barrier_semaphore()
+        for other in (self.x, self.y, self.sibling):
+            pl.semaphore_signal(barrier, inc=1, device_id=other, device_id_type=MESH)
+
+        @pl.when(self.has_left)
+        def _():
+            pl.semaphore_signal(barrier, inc=1, device_id=self.left, device_id_type=MESH)
+
+        @pl.when(self.has_right)
+        def _():
+            pl.semaphore_signal(barrier, inc=1, device_id=self.right, device_id_type=MESH)
+
+        lefts = lax.div(self.z + self.depth - 1, self.depth)
+        rights = lax.div(2 * (self.depth - 1) - self.z, self.depth)
+        pl.semaphore_wait(barrier, 3 + lefts + rights)
+
+    def at_distance(self, k):
+        if k == 0:
+            return [(None, self.z, 0)]
+        return [
+            (self.z >= k, self.z - k, -1),
+            (self.z + k < self.depth, self.z + k, 1),
+        ]
+
+    def send(self, when, make):
+        guarded(when, lambda: make().start())
+        self.pending.append((when, make))
+
+    def finish(self):
+        for when, make in self.pending:
+            guarded(when, lambda make=make: make().wait_send())
+
+
+def guarded(when, action):
+    if when is None:
+        action()
+    else:
+        pl.when(when)(action)
+
+
+def both_true(first, second):
+    return second if first is None else jnp.logical_and(first, second)
+
+
+def remote(src, dst, send_sem, recv_sem, device):
+    return pltpu.make_async_remote_copy(
+        src_ref=src,
+        dst_ref=dst,
+        send_sem=send_sem,
+        recv_sem=recv_sem,
+        device_id=device,
+        device_id_type=MESH,
+    )
+
+
+def gather_kernel(block_ref, out_ref, own_sem, sz, sx, sy, sa, sb, ss, rz, rx, ry, ra, rb, rs):
+    here = Around()
+    half = block_ref.shape[0] // 2
+    depth = here.depth
+
+    def place(dp, z, core):
+        return out_ref.at[(dp * depth + z) * 2 + core]
+
+    own = pltpu.make_async_copy(block_ref, place(here.dp, here.z, here.core), own_sem)
+    own.start()
+    here.greet()
+    halves = (pl.ds(0, half), pl.ds(half, half))
+
+    def full(dp, z, send_sem, recv_sem, device, mine=False):
+        spot = place(dp, z, here.core)
+        src = block_ref if mine else spot
+        return lambda: remote(src, spot, send_sem, recv_sem, device)
+
+    def part(dp, z, which, send_sem, recv_sem, device):
+        spot = place(dp, z, here.core).at[halves[which]]
+        return lambda: remote(spot, spot, send_sem, recv_sem, device)
+
+    def to_sibling(when, dp, z, mine=False):
+        n = dp * depth + z
+        here.send(when, full(dp, z, ss.at[n], rs.at[n], here.sibling, mine))
+
+    def along_z(k):
+        for when, z, side in here.at_distance(k):
+            mine = side == 0
+            if not mine:
+                guarded(when, lambda z=z: full(here.dp, z, sz.at[0, z], rz.at[z], here.left)().wait_recv())
+            if side <= 0:
+                here.send(
+                    both_true(when, here.has_right),
+                    full(here.dp, z, sz.at[1, z], rz.at[z], here.right, mine),
+                )
+            if side >= 0:
+                here.send(
+                    both_true(when, here.has_left),
+                    full(here.dp, z, sz.at[0, z], rz.at[z], here.left, mine),
+                )
+            here.send(when, full(here.dp, z, sx.at[z], rx.at[z], here.x, mine))
+            here.send(when, full(here.dp, z, sy.at[z], ry.at[z], here.y, mine))
+            to_sibling(when, here.dp, z, mine)
+
+    def turn(k):
+        for when, z, _ in here.at_distance(k):
+            guarded(when, lambda z=z: full(here.line, z, sx.at[z], rx.at[z], here.x)().wait_recv())
+            here.send(when, part(here.line, z, 0, sa.at[z], ra.at[z], here.y))
+            to_sibling(when, here.line, z)
+            guarded(when, lambda z=z: full(here.column, z, sy.at[z], ry.at[z], here.y)().wait_recv())
+            here.send(when, part(here.column, z, 1, sb.at[z], rb.at[z], here.x))
+            to_sibling(when, here.column, z)
+
+    def corner(k):
+        for when, z, _ in here.at_distance(k):
+            guarded(when, lambda z=z: part(here.corner, z, 0, sa.at[z], ra.at[z], here.y)().wait_recv())
+            guarded(when, lambda z=z: part(here.corner, z, 1, sb.at[z], rb.at[z], here.x)().wait_recv())
+            to_sibling(when, here.corner, z)
+
+    along_z(0)
+    for k in range(1, depth):
+        along_z(k)
+        turn(k - 1)
+        if k > 1:
+            corner(k - 2)
+    turn(depth - 1)
+    corner(depth - 2)
+    corner(depth - 1)
+
+    for n in range(4 * depth):
+        spot = out_ref.at[n * 2 + 1 - here.core]
+        remote(spot, spot, ss.at[n], rs.at[n], here.sibling).wait_recv()
+    here.finish()
+    own.wait()
+
+
 def collect(block):
-    return lax.all_gather(block, ("dp", "label"), axis=0, tiled=False)
+    depth = lax.axis_size("label") // 2
+    sems = pltpu.SemaphoreType.DMA
+    line = sems((depth,))
+    return pl.pallas_call(
+        gather_kernel,
+        in_specs=[pl.BlockSpec(memory_space=pl.ANY)],
+        out_specs=pl.BlockSpec(memory_space=pl.ANY),
+        out_shape=jax.ShapeDtypeStruct((8 * depth,) + block.shape, block.dtype),
+        scratch_shapes=[sems, sems((2, depth)), line, line, line, line, sems((4 * depth,))]
+        + [line, line, line, line, line, sems((4 * depth,))],
+        compiler_params=pltpu.CompilerParams(collective_id=0, has_side_effects=True),
+        name="gather_rows",
+    )(block)
+
+
+def scatter_kernel(part_ref, out_ref, arrived, acc, ina, inb, inx, iny, inz, total,
+                   sz, sx, sy, sa, sb, ss, rz, rx, ry, ra, rb, rs):
+    here = Around()
+    depth = here.depth
+    rows = out_ref.shape[0]
+    half = rows // 2
+    tile = 64 if half % 64 == 0 else 16
+    halves = (pl.ds(0, half), pl.ds(half, half))
+    here.greet()
+
+    def sibling_copy(n, core):
+        return remote(
+            part_ref.at[n * 2 + core], arrived.at[n], ss.at[n], rs.at[n], here.sibling
+        )
+
+    order = [here.corner, here.line, here.column, here.dp]
+    for k in range(depth - 1, -1, -1):
+        for when, z, _ in here.at_distance(k):
+            for dp in order:
+                here.send(
+                    when,
+                    lambda n=dp * depth + z: sibling_copy(n, 1 - here.core),
+                )
+
+    def add(dst, first, others, start=0, count=rows):
+        @pl.loop(0, count // tile)
+        def _(i):
+            at = pl.ds(pl.multiple_of(i * tile, tile) + start, tile)
+            inner = pl.ds(pl.multiple_of(i * tile, tile), tile)
+            value = first[at, :].astype(jnp.float32)
+            for other in others:
+                value = value + other[inner, :].astype(jnp.float32)
+            dst[at, :] = value.astype(dst.dtype)
+
+    def send_a(z):
+        n = here.corner * depth + z
+        return remote(acc.at[n, halves[0]], ina.at[z], sa.at[z], ra.at[z], here.y)
+
+    def send_b(z):
+        n = here.corner * depth + z
+        return remote(acc.at[n, halves[1]], inb.at[z], sb.at[z], rb.at[z], here.x)
+
+    def send_x(z):
+        return remote(acc.at[here.line * depth + z], inx.at[z], sx.at[z], rx.at[z], here.x)
+
+    def send_y(z):
+        return remote(acc.at[here.column * depth + z], iny.at[z], sy.at[z], ry.at[z], here.y)
+
+    def send_right(z):
+        return remote(total.at[z], inz.at[0, z], sz.at[0, z], rz.at[0, z], here.right)
+
+    def send_left(z):
+        return remote(total.at[z], inz.at[1, z], sz.at[1, z], rz.at[1, z], here.left)
+
+    def cores(k):
+        for when, z, _ in here.at_distance(k):
+            for dp in order:
+
+                def one(n=dp * depth + z):
+                    sibling_copy(n, 1 - here.core).wait_recv()
+                    add(acc.at[n], part_ref.at[n * 2 + here.core], [arrived.at[n]])
+
+                guarded(when, one)
+                if dp is here.corner:
+                    here.send(when, lambda z=z: send_a(z))
+                    here.send(when, lambda z=z: send_b(z))
+
+    def turn(k):
+        for when, z, _ in here.at_distance(k):
+
+            def first(z=z):
+                send_a(z).wait_recv()
+                spot = acc.at[here.line * depth + z]
+                add(spot, spot, [ina.at[z]], 0, half)
+
+            guarded(when, first)
+            here.send(when, lambda z=z: send_x(z))
+
+            def second(z=z):
+                send_b(z).wait_recv()
+                spot = acc.at[here.column * depth + z]
+                add(spot, spot, [inb.at[z]], half, half)
+
+            guarded(when, second)
+            here.send(when, lambda z=z: send_y(z))
+
+    def along_z(k):
+        for when, z, side in here.at_distance(k):
+
+            def quad(z=z):
+                send_x(z).wait_recv()
+                send_y(z).wait_recv()
+                dst = out_ref if side == 0 else total.at[z]
+                add(dst, acc.at[here.dp * depth + z], [inx.at[z], iny.at[z]])
+
+            guarded(when, quad)
+            dst = out_ref if side == 0 else total.at[z]
+            if side >= 0:
+
+                def from_left(z=z, dst=dst):
+                    send_right(z).wait_recv()
+                    add(dst, dst, [inz.at[0, z]])
+
+                guarded(both_true(when, here.has_left), from_left)
+            if side <= 0:
+
+                def from_right(z=z, dst=dst):
+                    send_left(z).wait_recv()
+                    add(dst, dst, [inz.at[1, z]])
+
+                guarded(both_true(when, here.has_right), from_right)
+            if side > 0:
+                here.send(when, lambda z=z: send_right(z))
+            if side < 0:
+                here.send(when, lambda z=z: send_left(z))
+
+    far = depth - 1
+    for step in range(depth + 2):
+        if step < depth:
+            cores(far - step)
+        if 0 <= step - 1 < depth:
+            turn(far - step + 1)
+        if 0 <= step - 2 < depth:
+            along_z(far - step + 2)
+    here.finish()
 
 
 def send_back(part):
-    return lax.psum_scatter(part, ("dp", "label"), scatter_dimension=0, tiled=False)
+    depth = lax.axis_size("label") // 2
+    _, rows, features = part.shape
+    sems = pltpu.SemaphoreType.DMA
+    line = sems((depth,))
+    kind = part.dtype
+    return pl.pallas_call(
+        scatter_kernel,
+        in_specs=[pl.BlockSpec(memory_space=pltpu.VMEM)],
+        out_specs=pl.BlockSpec(memory_space=pltpu.VMEM),
+        out_shape=jax.ShapeDtypeStruct((rows, features), jnp.float32),
+        scratch_shapes=[
+            pltpu.VMEM((4 * depth, rows, features), kind),
+            pltpu.VMEM((4 * depth, rows, features), kind),
+            pltpu.VMEM((depth, rows // 2, features), kind),
+            pltpu.VMEM((depth, rows // 2, features), kind),
+            pltpu.VMEM((depth, rows, features), kind),
+            pltpu.VMEM((depth, rows, features), kind),
+            pltpu.VMEM((2, depth, rows, features), kind),
+            pltpu.VMEM((depth, rows, features), kind),
+        ]
+        + [sems((2, depth)), line, line, line, line, sems((4 * depth,))]
+        + [sems((2, depth)), line, line, line, line, sems((4 * depth,))],
+        compiler_params=pltpu.CompilerParams(
+            collective_id=1, has_side_effects=True, vmem_limit_bytes=56 * 1024 * 1024
+        ),
+        name="return_rows",
+    )(part)
 
 
 def per_device(encoded, coarse_weight, fine_weight, cluster_group, cluster_member, positive):

time: 339 us -> 188 us (0.55)
  waiting for transfers between devices: 257 us -> 0 us
  Pallas kernels: 58.2 us -> 177 us
  between operations: 14.1 us -> 0.69 us
    reduce_scatter x1 -> x0, waiting for transfers between devices: 150 us -> none  [send_back(): lax.psum_scatter(part, ('dp', 'label'), scatter_dimension=0, tiled=False)]
    pallas_call x0 -> x2, Pallas kernels: none -> 128 us  [the longest x1 66.4 us: collect(): pl.pallas_call(gather_kernel, in_specs=[pl.BlockSpec(memory_space=pl.ANY)...]
    all_gather x1 -> x0, waiting for transfers between devices: 106 us -> none  [collect(): return lax.all_gather(block, ('dp', 'label'), axis=0, tiled=False)]
    pallas_call x1, Pallas kernels: 58.2 us -> 48.5 us  [fine_part(): pl.pallas_call(functools.partial(fine_kernel, capacity, labels), grid=(de...]
  transfers between devices with their start and end apart: 2 -> 0, of which waited for: 2 -> 0; matrix products, arithmetic and copies ran while one was open for 1% -> 0% of each run, Pallas kernels for 0% -> 0%
where the time goes in v2:
time: 188 us; the launch traced here: 187 us
  Pallas kernels  177 us (94%)
  other arithmetic  5.39 us (3%)
  matrix products  2.71 us (1%)
    pallas_call x1, Pallas kernels, collect(): pl.pallas_call(gather_kernel, in_specs=[pl.BlockSpec(memory_space=pl.ANY)...  66.4 us
    pallas_call x1, Pallas kernels, send_back(): pl.pallas_call(scatter_kernel, in_specs=[pl.BlockSpec(memory_space=pltpu....  61.9 us
    pallas_call x1, Pallas kernels, fine_part(): pl.pallas_call(functools.partial(fine_kernel, capacity, labels), grid=(de...  48.5 us

profile of v2, /device:TPU:0, one launch (start us, length us, event | category | flops | bytes accessed | tf_op | source)
XLA Modules:
  0.0 187.2 jit_solution(13253555306563637832)
XLA Ops:
  0.6 0.0 copy-start
  0.6 0.7 convert.14
  1.4 0.7 slice_add_fusion
  2.1 0.7 convert_bitcast_fusion
  2.8 0.7 fusion.12.upper_ref
  3.5 1.8 fusion.8.block_ref
  5.3 66.4 %gather_rows.1.gathered_ref = bf16[32,288,768]{2,1,0:T(8,128)(2,1)} custom-call(bf16[288,768]{1,0:T(8,128)(2,1)} %fusion.8.block_ref), custom_call_target="tpu_custom_call" | custom-call | tf_op jit(solution)/shard_map/gather_rows/pallas_call | solution.py:522
  71.7 1.2 slice.12
  72.9 0.0 copy-done
  72.9 0.4 fusion.14
  73.3 0.2 fusion.4
  73.5 0.6 fusion.13
  74.1 48.5 %fine_part.1 = (bf16[32,256,768]{2,1,0:T(8,128)(2,1)}, bf16[2048,768]{1,0:T(8,128)(2,1)}, f32[1,128]{1,0:T(1,128)}) custom-call(s32[1]{0:T(128)} %bitcast.5.me_ref, bf16[256,256]{1,0:T(8,128)(2,1)} %fusion.12.upper_ref, bf16[32,288,768]{2,1,0:T(8,128)(2,1)} %gather_rows.1.gathered_ref, bf16[2048,768]{1,0:T(8,128)(2,1)} %bitcast.33), custom_call_target="tpu_custom_call" | custom-call | tf_op jit(solution)/shard_map/fine_part/pallas_call | solution.py:293
  122.5 0.0 copy-start.1
  122.5 61.9 %return_rows.1 = f32[256,768]{1,0:T(8,128)} custom-call(bf16[32,256,768]{2,1,0:T(8,128)(2,1)} %get-tuple-element.7.part_ref), custom_call_target="tpu_custom_call" | custom-call | tf_op jit(solution)/shard_map/return_rows/pallas_call | solution.py:667
  184.4 2.3 %fusion = bf16[256,768]{1,0:T(8,128)(2,1)} fusion(f32[256,768]{1,0:T(8,128)} %return_rows.1, bf16[512,768]{1,0:T(8,128)(2,1)S(1)} %bitcast.32, f32[512,256]{1,0:T(8,128)S(1)} %get-tuple-element.15, f32[256]{0:T(256)S(1)} %get-tuple-element.13, s32[256]{0:T(256)S(1)} %bitcast.35), kind=kOutput, calls=%fused_computation.1 | convolution fusion | flops 202375168 | bytes 2492416 | tf_op jit(solution)/shard_map/dot_general | solution.py:358
  186.7 0.0 copy-done.1
  186.7 0.5 slice_bitcast_fusion
  (2 shorter events, 0.0 us)
Async XLA Ops:
  0.6 72.3 %copy-start = (bf16[256,768]{1,0:T(8,128)(2,1)S(1)}, bf16[256,768]{1,0:T(8,128)(2,1)}, u32[]{:S(2)}) copy-start(bf16[256,768]{1,0:T(8,128)(2,1)} %param.6) | copy-start | bytes 1179652
  122.5 64.2 %copy-start.1 = (f32[1,128]{1,0:T(1,128)S(1)}, f32[1,128]{1,0:T(1,128)}, u32[]{:S(2)}) copy-start(f32[1,128]{1,0:T(1,128)} %get-tuple-element.9) | copy-start | bytes 1540
